TPU v7x, 32 devices: a whole 2x2x4 slice. The times are simulated.
32 devices in a mesh: head: 4 (over y, x), seq: 8 (over z, core).
Axes of the slice: x: 2, y: 2, z: 4, core: 2. Of those that a mesh axis runs over, the one named last changes fastest.
Arguments:
- q_nope: bfloat16 [1024, 16384], P('seq', 'head'), may hold values from -6 to 6
- q_rope: bfloat16 [1024, 8192], P('seq', 'head'), may hold values from -128 to 128
- kv_latent: bfloat16 [1024, 576], P('seq'), may hold values from -10 to 10
- group_ids: int32 [1024], replicated, may hold values from 0 to 15, never falling along the last dimension, each value on 1 to 128 neighbouring positions
- w_uk: bfloat16 [128, 128, 512], P('head'), may hold values from -0.5 to 0.5
- w_uv: bfloat16 [128, 512, 128], P('head'), may hold values from -0.25 to 0.25
- moe_in: bfloat16 [2048, 7168], P('seq', 'head'), may hold values from -6 to 6
- expert_ids: int32 [2048, 2], P('seq'), may hold values from 0 to 7, all different within a row; in each aligned block of 256 rows (0 to 255, 256 to 511, ...) at most 128 rows name the same one
- gate_w: float32 [2048, 2], P('seq'), may hold values from 0.1 to 1
- w_gate: bfloat16 [8, 7168, 1024], P('seq', 'head'), may hold values from -0.0625 to 0.0625
- w_up: bfloat16 [8, 7168, 1024], P('seq', 'head'), may hold values from -0.0625 to 0.0625
- w_down: bfloat16 [8, 1024, 7168], P('seq', None, 'head'), may hold values from -0.1875 to 0.1875
Outputs:
- attn_out: bfloat16 [1024, 16384], P('seq', 'head')
- moe_out: bfloat16 [2048, 7168], P('seq', 'head')
Inputs may be any that keep to these rules, and one draw needn't show every extreme that they name: `expert_ids`: each row names 2 different experts. Among the routes of one aligned block of 256 rows (the rows of one index of seq) no expert is named more than 128 times, a bound that some block reaches. `group_ids`: never falls along the rows; each group holds 1 to 128 consecutive tokens, one exactly 128.
All inputs are finite; a program needn't handle non-finite values.
Results may differ from a plain program's by a relative error of at most 0.007.
Values may be sent and summed in bfloat16 or wider, within the bound.
A program may use at most 192 MiB of HBM per device.

v0:
```python
import jax
import jax.numpy as jnp
from jax import lax
from jax.sharding import PartitionSpec as P


def passed_along(value, axis, steps):
    count = lax.axis_size(axis)
    initial, last = (max(0, -steps), min(count, count - steps))
    return lax.ppermute(value, axis, [(source, source + steps) for source in range(initial, last)])


def attend_local(query_nope, query_rope, all_keys, key_ids, query_ids, w_uk, w_uv):
    tok_count = query_nope.shape[0]
    head_count = w_uk.shape[0]
    nope_width = w_uk.shape[1]
    lat_width = w_uk.shape[2]
    rope_width = query_rope.shape[1] // head_count
    q_split = query_nope.reshape(tok_count, head_count, nope_width)
    r_split = query_rope.reshape(tok_count, head_count, rope_width)
    q_latent = jnp.einsum("thn,hnl->htl", q_split, w_uk, preferred_element_type=jnp.float32).astype(
        jnp.bfloat16
    )
    latent = all_keys[:, :lat_width]
    rotary = all_keys[:, lat_width:]
    scale_factor = (nope_width + rope_width) ** (-0.5)
    scores = jnp.einsum("htl,kl->htk", q_latent, latent, preferred_element_type=jnp.float32)
    scores = (
        scores + jnp.einsum("thr,kr->htk", r_split, rotary, preferred_element_type=jnp.float32)
    ) * scale_factor
    key_count = all_keys.shape[0]
    query_pos = jnp.arange(tok_count, dtype=jnp.int32) + (key_count - tok_count)
    key_pos = jnp.arange(key_count, dtype=jnp.int32)
    allowed = (key_ids[None, :] == query_ids[:, None]) & (key_pos[None, :] <= query_pos[:, None])
    scores = jnp.where(allowed[None], scores, -jnp.inf)
    highest = jnp.max(scores, axis=2, keepdims=True)
    expo = jnp.exp(scores - highest)
    probs = (expo / jnp.sum(expo, axis=2, keepdims=True)).astype(jnp.bfloat16)
    mixed_latent = jnp.einsum(
        "htk,kl->htl", probs, latent, preferred_element_type=jnp.float32
    ).astype(jnp.bfloat16)
    heads_out = jnp.einsum("htl,hlv->thv", mixed_latent, w_uv, preferred_element_type=jnp.float32)
    return heads_out.astype(jnp.bfloat16).reshape(tok_count, head_count * w_uv.shape[2])


def on_device(
    q_nope,
    q_rope,
    kv_latent,
    group_ids,
    w_uk,
    w_uv,
    moe_in,
    expert_ids,
    gate_w,
    w_gate,
    w_up,
    w_down,
):
    att_rows = kv_latent.shape[0]
    earlier = passed_along(kv_latent, "seq", 1)
    all_keys = jnp.concatenate([earlier, kv_latent], axis=0)
    padded_ids = jnp.concatenate([jnp.full((att_rows,), -1, jnp.int32), group_ids])
    row_start = lax.axis_index("seq") * att_rows
    key_ids = lax.dynamic_slice_in_dim(padded_ids, row_start, 2 * att_rows, 0)
    query_ids = lax.dynamic_slice_in_dim(group_ids, row_start, att_rows, 0)
    tokens_here = moe_in.shape[0]
    feat_width = moe_in.shape[1]
    top_count = expert_ids.shape[1]
    expert_count = lax.axis_size("seq")
    capacity = 2 * tokens_here * top_count // expert_count
    flat_ids = expert_ids.reshape(-1)
    onehot = (flat_ids[:, None] == jnp.arange(expert_count, dtype=jnp.int32)[None, :]).astype(
        jnp.int32
    )
    before = jnp.cumsum(onehot, axis=0) - onehot
    slot_of = jnp.sum(before * onehot, axis=1)
    target = flat_ids * capacity + slot_of
    placing = (
        jnp.arange(expert_count * capacity, dtype=jnp.int32)[:, None] == target[None, :]
    ).astype(jnp.bfloat16)
    to_token = jnp.sum(placing.reshape(expert_count * capacity, tokens_here, top_count), axis=2)
    outgoing = jnp.dot(to_token, moe_in, preferred_element_type=jnp.float32).astype(jnp.bfloat16)
    outgoing = outgoing.reshape(expert_count, capacity, feat_width)
    gate_local = w_gate[0]
    up_local = w_up[0]
    down_local = w_down[0]
    arrived = lax.all_to_all(outgoing, "seq", split_axis=0, concat_axis=0, tiled=True)
    sources, items, width = arrived.shape
    row_block = arrived.reshape(sources * items, width)
    gate_part = jnp.dot(row_block, gate_local, preferred_element_type=jnp.float32)
    up_part = jnp.dot(row_block, up_local, preferred_element_type=jnp.float32)
    gate_sum = lax.psum_scatter(gate_part, "head", scatter_dimension=1, tiled=True)
    up_sum = lax.psum_scatter(up_part, "head", scatter_dimension=1, tiled=True)
    hidden_part = (jax.nn.silu(gate_sum) * up_sum).astype(jnp.bfloat16)
    hidden = lax.all_gather(hidden_part, "head", axis=1, tiled=True)
    result = jnp.dot(hidden, down_local, preferred_element_type=jnp.float32).astype(jnp.bfloat16)
    processed = result.reshape(sources, items, width)
    attn_out = attend_local(q_nope, q_rope, all_keys, key_ids, query_ids, w_uk, w_uv)
    returned = lax.all_to_all(processed, "seq", split_axis=0, concat_axis=0, tiled=True)
    picked = jnp.einsum(
        "pr,pw->rw",
        placing,
        returned.reshape(expert_count * capacity, feat_width),
        preferred_element_type=jnp.float32,
    )
    picked = picked.reshape(tokens_here, top_count, feat_width)
    mixed = jnp.sum(gate_w[:, :, None] * picked, axis=1)
    moe_out = (moe_in.astype(jnp.float32) + mixed).astype(jnp.bfloat16)
    return (attn_out, moe_out)


def solution(mesh):
    return jax.shard_map(
        on_device,
        mesh=mesh,
        in_specs=(
            P("seq", "head"),
            P("seq", "head"),
            P("seq", None),
            P(),
            P("head", None, None),
            P("head", None, None),
            P("seq", "head"),
            P("seq", None),
            P("seq", None),
            P("seq", "head", None),
            P("seq", "head", None),
            P("seq", None, "head"),
        ),
        out_specs=(P("seq", "head"), P("seq", "head")),
        check_vma=False,
    )
```

profile of v0, /device:TPU:16, one launch (start us, length us, event | category | flops | bytes accessed | tf_op | source)
XLA Modules:
  0.0 391.8 jit_solution(9490008380932152020)
XLA Ops:
  7.2 0.0 copy-start
  7.2 0.0 reduce-scatter.3.cloned.1.call-start
  7.2 0.9 copy.55
  8.1 0.1 eq.76
  8.3 0.1 reshape.146
  8.4 1.1 reduce-window.6
  9.6 0.2 slice_reduce_fusion
  9.8 0.1 fusion.41
  9.9 0.1 reduce_sum.43
  10.1 0.1 copy.57
  10.1 0.7 multiply_add_fusion
  10.8 0.5 fusion.25
  11.3 2.3 convolution_convert_fusion
  13.6 0.0 copy-start.6
  13.6 84.7 %all_to_all.10 = bf16[8,128,1792]{2,1,0:T(8,128)(2,1)S(1)} all-to-all(bf16[8,128,1792]{2,1,0:T(8,128)(2,1)S(1)} %bitcast.61), channel_id=1, replica_groups=mesh['head'=4,'seq'=8] {'seq'}, dimensions={0} | all-to-all | bytes 7340032 | tf_op jit(solution)/shard_map/all_to_all | solution.py:88
  98.4 1.9 copy-done.1
  100.2 0.0 copy-done.6
  100.2 5.5 %fusion.10 = f32[1024,1024]{1,0:T(8,128)} fusion(bf16[1024,1792]{1,0:T(8,128)(2,1)S(1)} %bitcast.63, bf16[1,1792,1024]{2,1,0:T(8,128)(2,1)S(1)} %copy-done.6), kind=kOutput, calls=%fused_computation.15 | convolution fusion | flops 3758096384 | bytes 11534336 | tf_op jit(solution)/shard_map/dot_general | solution.py:91
  105.7 0.0 reduce-scatter.3.cloned.1.call-update
  105.8 0.0 reduce-scatter.5.cloned.1.call-start
  105.8 9.2 %fusion.8 = f32[1024,1024]{1,0:T(8,128)} fusion(bf16[1024,1792]{1,0:T(8,128)(2,1)} %bitcast.64, bf16[1,1792,1024]{2,1,0:T(8,128)(2,1)} %param.22), kind=kOutput, calls=%fused_computation.13 | convolution fusion | flops 3758096384 | bytes 11534336 | tf_op jit(solution)/shard_map/dot_general | solution.py:92
  115.0 0.0 reduce-scatter.5.cloned.1.call-update
  115.0 0.0 all-gather.2.cloned.1.call-start
  115.1 45.2 %reduce-scatter.3.cloned.1.call-done = f32[1024,256]{1,0:T(8,128)} async-done(((f32[1024,1024]{1,0:T(8,128)}), f32[1024,256]{1,0:T(8,128)}) %reduce-scatter.3.cloned.1.call-update) | async-done | bytes 1048592 | tf_op jit(solution)/shard_map/reduce_scatter | solution.py:93
  160.3 55.9 %reduce-scatter.5.cloned.1.call-done = f32[1024,256]{1,0:T(8,128)} async-done(((f32[1024,1024]{1,0:T(8,128)}), f32[1024,256]{1,0:T(8,128)}) %reduce-scatter.5.cloned.1.call-update) | async-done | bytes 1048592 | tf_op jit(solution)/shard_map/reduce_scatter | solution.py:94
  216.2 2.6 multiply_convert_fusion
  218.8 0.0 all-gather.2.cloned.1.call-update
  218.8 35.3 %all-gather.2.cloned.1.call-done = bf16[1024,1024]{1,0:T(8,128)(2,1)} async-done(((bf16[1024,256]{1,0:T(8,128)(2,1)}), bf16[1024,1024]{1,0:T(8,128)(2,1)}) %all-gather.2.cloned.1.call-update) | async-done | bytes 2097168 | tf_op jit(solution)/shard_map/all_gather | solution.py:96
  254.2 8.5 %convolution_convert_fusion.1 = bf16[1024,1792]{1,0:T(8,128)(2,1)} fusion(bf16[1024,1024]{1,0:T(8,128)(2,1)} %all-gather.2.cloned.1.call-done, bf16[1,1024,1792]{2,1,0:T(8,128)(2,1)} %param.23), kind=kOutput, calls=%fused_computation.11 | convolution fusion | flops 3759931392 | bytes 9437184 | tf_op jit(solution)/shard_map/dot_general | solution.py:97
  262.6 5.2 %all-to-all-start.1 = ((bf16[8,128,1792]{2,1,0:T(8,128)(2,1)}), bf16[8,128,1792]{2,1,0:T(8,128)(2,1)}, u32[]{:S(2)}, u32[]{:S(2)}) async-start(bf16[8,128,1792]{2,1,0:T(8,128)(2,1)} %bitcast.62), calls=%async_computation.3 | async-start | bytes 7340032 | tf_op jit(solution)/shard_map/all_to_all | solution.py:100
  267.9 0.2 copy.49
  268.0 2.2 collective-permute-start
  270.3 0.3 copy.51
  270.6 0.4 iota_compare_fusion.1
  271.0 1.0 eq.82
  271.9 0.1 dynamic_slice.7
  272.0 0.1 pad_dynamic-slice_fusion
  272.1 0.1 fusion.32
  272.2 77.6 %collective-permute-done = bf16[128,576]{1,0:T(8,128)(2,1)S(1)} collective-permute-done((bf16[128,576]{1,0:T(8,128)(2,1)S(1)}, bf16[128,576]{1,0:T(8,128)(2,1)S(1)}, u32[]{:S(2)}, u32[]{:S(2)}) %collective-permute-start) | collective-permute-done | bytes 147488 | tf_op jit(solution)/shard_map/ppermute | solution.py:10
  349.8 2.7 fusion.34
  352.5 7.8 %fusion.2 = f32[32,128,256]{2,1,0:T(8,128)} fusion(f32[256,128,32]{0,1,2:T(8,128)} %fusion.34, bf16[32,128,512]{2,1,0:T(8,128)(2,1)} %param.16, pred[128,256]{1,0:T(8,128)(4,1)S(1)} %fusion.32, bf16[128,576]{1,0:T(8,128)(2,1)S(1)} %collective-permute-done, bf16[128,576]{1,0:T(8,128)(2,1)S(1)} %copy.49, bf16[128,4096]{1,0:T(8,128)(2,1)S(1)} %copy-done), kind=kOutput, calls=%fused_computation.3 | convolution fusion | flops 1616379904 | bytes 13959168 | tf_op jit(solution)/shard_map/htl,kl->htk/dot_general | solution.py:27
  360.3 4.6 %fusion.49 = f32[32,128]{1,0:T(8,128)S(1)} fusion(f32[32,128,256]{2,1,0:T(8,128)} %fusion.2), kind=kOutput, calls=%fused_computation.56 | output fusion | flops 2097407 | bytes 4210688 | tf_op jit(solution)/shard_map/sub | solution.py:37
  365.0 0.0 copy-start.7
  365.0 13.2 %fusion.22 = bf16[32,128,128]{1,2,0:T(8,128)(2,1)S(1)} fusion(bf16[32,512,128]{2,1,0:T(8,128)(2,1)} %param.17, f32[32,128]{1,0:T(8,128)S(1)} %fusion.49, f32[32,128,256]{2,1,0:T(8,128)} %fusion.2, bf16[128,576]{1,0:T(8,128)(2,1)S(1)} %collective-permute-done, bf16[128,576]{1,0:T(8,128)(2,1)S(1)} %copy.49), kind=kOutput, calls=%fused_computation.26 | convolution fusion | flops 1616908544 | bytes 13942784 | tf_op jit(solution)/shard_map/htl,hlv->thv/dot_general | solution.py:42
  378.2 1.3 copy.59
  379.5 0.0 all-to-all-done.1
  379.5 4.6 %multiply_reduce_fusion = f32[256,1792]{1,0:T(8,128)S(1)} fusion(bf16[1024,1792,1]{1,0,2:T(8,128)(2,1)} %bitcast.15, pred[256,2,1024]{2,1,0:T(4,128)(4,1)S(1)} %eq.82, f32[256,2]{0,1:T(2,128)S(1)} %copy-done.7), kind=kOutput, calls=%fused_computation.17 | convolution fusion | flops 1880424448 | bytes 6031360 | tf_op jit(solution)/shard_map/pr,pw->rw/dot_general | solution.py:101
  384.1 1.1 add_convert_fusion
  (16 shorter events, 0.1 us)
Async XLA Ops:
  7.2 345.4 %copy-start = (bf16[128,4096]{1,0:T(8,128)(2,1)S(1)}, bf16[128,4096]{1,0:T(8,128)(2,1)}, u32[]{:S(2)}) copy-start(bf16[128,4096]{1,0:T(8,128)(2,1)} %param.12) | copy-start | bytes 3145732
  7.2 153.1 %reduce-scatter.3.cloned.1.call-start = ((), (), s32[]{:S(2)}) async-start(), calls=%async_computation.4 | async-start | bytes 5242880 | tf_op jit(solution)/shard_map/reduce_scatter | solution.py:93
  13.6 86.6 %copy-start.6 = (bf16[1,1792,1024]{2,1,0:T(8,128)(2,1)S(1)}, bf16[1,1792,1024]{2,1,0:T(8,128)(2,1)}, u32[]{:S(2)}) copy-start(bf16[1,1792,1024]{2,1,0:T(8,128)(2,1)} %param.21) | copy-start | bytes 11010052
  98.4 1.9 copy-start.1
  105.8 110.4 %reduce-scatter.5.cloned.1.call-start = ((), (), s32[]{:S(2)}) async-start(), calls=%async_computation.5 | async-start | bytes 5242880 | tf_op jit(solution)/shard_map/reduce_scatter | solution.py:94
  115.0 139.1 %all-gather.2.cloned.1.call-start = ((), (), s32[]{:S(2)}) async-start(), calls=%async_computation.6 | async-start | bytes 2621440 | tf_op jit(solution)/shard_map/all_gather | solution.py:96
  262.6 5.3 %copy-start.4 = (bf16[128,576]{0,1:T(8,128)(2,1)S(1)}, bf16[128,576]{0,1:T(8,128)(2,1)}, u32[]{:S(2)}) copy-start(bf16[128,576]{0,1:T(8,128)(2,1)} %param.14) | copy-start | bytes 442372
  262.6 7.7 %copy-start.3 = (bf16[128,2048]{1,0:T(8,128)(2,1)S(1)}, bf16[128,2048]{1,0:T(8,128)(2,1)}, u32[]{:S(2)}) copy-start(bf16[128,2048]{1,0:T(8,128)(2,1)} %param.13) | copy-start | bytes 1572868
  262.6 9.3 %copy-start.5 = (s32[1024]{0:T(1024)S(1)}, s32[1024]{0:T(1024)}, u32[]{:S(2)}) copy-start(s32[1024]{0:T(1024)} %param.15) | copy-start | bytes 12292
  262.6 116.9 %all-to-all-start.1 = ((bf16[8,128,1792]{2,1,0:T(8,128)(2,1)}), bf16[8,128,1792]{2,1,0:T(8,128)(2,1)}, u32[]{:S(2)}, u32[]{:S(2)}) async-start(bf16[8,128,1792]{2,1,0:T(8,128)(2,1)} %bitcast.62), calls=%async_computation.3 | async-start | bytes 7340032 | tf_op jit(solution)/shard_map/all_to_all | solution.py:100
  268.0 81.8 %collective-permute-start = (bf16[128,576]{1,0:T(8,128)(2,1)S(1)}, bf16[128,576]{1,0:T(8,128)(2,1)S(1)}, u32[]{:S(2)}, u32[]{:S(2)}) collective-permute-start(bf16[128,576]{1,0:T(8,128)(2,1)S(1)} %copy.49), channel_id=1, source_target_pairs={{0,1},{1,2},{2,3},{3,4},{4,5},{5,6},{6,7},{8,9},{9,10},{10,11},{11... | collective-permute-start | bytes 442376 | tf_op jit(solution)/shard_map/ppermute | solution.py:10
  365.0 14.6 %copy-start.7 = (f32[256,2]{0,1:T(2,128)S(1)}, f32[256,2]{0,1:T(2,128)}, u32[]{:S(2)}) copy-start(f32[256,2]{0,1:T(2,128)} %param.20) | copy-start | bytes 6148
  379.5 4.6 %copy-start.2 = (bf16[256,1792]{1,0:T(8,128)(2,1)S(1)}, bf16[256,1792]{1,0:T(8,128)(2,1)}, u32[]{:S(2)}) copy-start(bf16[256,1792]{1,0:T(8,128)(2,1)} %param.18) | copy-start | bytes 2752516
Sparse Core Ops, SparseCore 0:
  105.9 54.3 reduce-scatter.2
  163.5 52.6 reduce-scatter.4
  219.0 35.1 all-gather.1
where the time goes:
time: 392 us
  waiting for transfers between devices  214 us (55%)
  blocking collectives  84.7 us (22%)
  matrix products  53.7 us (14%)
  between operations  13.9 us (4%)
  other arithmetic  11.3 us (3%)
  starting transfers between devices  7.61 us (2%)
  local copies, waits for them, and re-layouts  6.39 us (2%)
    all_to_all x1, blocking collectives, on_device(): lax.all_to_all(outgoing, 'seq', split_axis=0, concat_axis=0, tiled=True)  84.7 us
    ppermute x1, waiting for transfers between devices, passed_along(): lax.ppermute(value, axis, [(source, source + steps) for source in range(i...  77.6 us
    reduce_scatter x1, waiting for transfers between devices, on_device(): up_sum = lax.psum_scatter(up_part, 'head', scatter_dimension=1, tiled=True)  55.9 us
    reduce_scatter x1, waiting for transfers between devices, on_device(): lax.psum_scatter(gate_part, 'head', scatter_dimension=1, tiled=True)  45.2 us
    all_gather x1, waiting for transfers between devices, on_device(): hidden = lax.all_gather(hidden_part, 'head', axis=1, tiled=True)  35.3 us
    dot_general x1, matrix products, attend_local(): jnp.einsum('htl,hlv->thv', mixed_latent, w_uv, preferred_element_type=jnp...  13.2 us
    dot_general x1, matrix products, on_device(): up_part = jnp.dot(row_block, up_local, preferred_element_type=jnp.float32)  9.19 us
    dot_general x1, matrix products, on_device(): jnp.dot(hidden, down_local, preferred_element_type=jnp.float32)  8.45 us
  transfers between devices with their start and end apart: 5, of which 4 were waited for; matrix products, arithmetic and copies ran while one was open for 10% of the time, Pallas kernels for 0%

commit v1 on v0

--- a/solution.py
+++ b/solution.py
@@ -1,6 +1,9 @@
+import functools
 import jax
 import jax.numpy as jnp
 from jax import lax
+from jax.experimental import pallas as pl
+from jax.experimental.pallas import tpu as pltpu
 from jax.sharding import PartitionSpec as P
 
 
@@ -43,6 +46,316 @@
     return heads_out.astype(jnp.bfloat16).reshape(tok_count, head_count * w_uv.shape[2])
 
 
+CHAIN_PARTS = 4
+F32, BF16 = jnp.float32, jnp.bfloat16
+
+
+def experts_kernel(sizes, x_ref, wg_hbm, wu_hbm, wd_hbm, out_ref, wg, wu, wd, xb, rows_out, rows_in, gu, gu_in,
+                   hid, back_out, back_in, near, contrib, acc_in, acc_out, load_sem, x_send, x_recv, swap_send,
+                   swap_recv, gu_send, gu_recv, hid_send, hid_recv, back_send, back_recv, acc_send, acc_recv):
+    tokens, width, capacity, part = sizes
+    s = lax.axis_index("seq")
+    h = lax.axis_index("head")
+    z, core = s // 2, s % 2
+    mate = s + 1 - 2 * core
+    edge = (z == 0) | (z == 3)
+    middle = (z == 1) | (z == 2)
+    inner_z = jnp.where(z == 0, 1, jnp.where(z == 3, 2, jnp.where(z == 1, 2, 1)))
+    inner = inner_z * 2 + core
+    outer = jnp.where(z <= 1, 0, 3) * 2 + core
+    peers = [jnp.where(h % 2 == 0, h + 1, h - 1), (h + 2) % 4, 3 - h]
+
+    loads = []
+    for at, (source, target) in enumerate(((wg_hbm, wg), (wu_hbm, wu), (wd_hbm, wd))):
+        copy = pltpu.make_async_copy(source, target, load_sem.at[at])
+        copy.start()
+        loads.append(copy)
+
+    barrier = pltpu.get_barrier_semaphore()
+    pl.semaphore_signal(barrier, inc=1, device_id={"seq": mate}, device_id_type=pl.DeviceIdType.MESH)
+    pl.semaphore_signal(barrier, inc=1, device_id={"seq": inner}, device_id_type=pl.DeviceIdType.MESH)
+    for peer in peers:
+        pl.semaphore_signal(barrier, inc=1, device_id={"head": peer}, device_id_type=pl.DeviceIdType.MESH)
+
+    @pl.when(middle)
+    def _():
+        pl.semaphore_signal(barrier, inc=1, device_id={"seq": outer}, device_id_type=pl.DeviceIdType.MESH)
+
+    @pl.when(middle)
+    def _():
+        pl.semaphore_wait(barrier, 6)
+
+    @pl.when(edge)
+    def _():
+        pl.semaphore_wait(barrier, 5)
+
+    def remote(source, target, send, recv, **device):
+        return pltpu.make_async_remote_copy(
+            src_ref=source, dst_ref=target, send_sem=send, recv_sem=recv, device_id=device,
+            device_id_type=pl.DeviceIdType.MESH,
+        )
+
+    sent = []
+
+    def send_when(condition, copy):
+        pl.when(condition)(copy.start)
+        sent.append((condition, copy))
+
+    def send(copy):
+        copy.start()
+        sent.append((None, copy))
+
+    send_when((z == 0) | middle, remote(x_ref, xb.at[1], x_send.at[0], x_recv.at[1],
+                                        seq=jnp.where(z == 0, inner, outer)))
+    send_when(z == 1, remote(x_ref, xb.at[1], x_send.at[1], x_recv.at[1], seq=inner))
+    send_when((z == 2) | (z == 3), remote(x_ref, xb.at[2], x_send.at[1], x_recv.at[2], seq=inner))
+
+    def x_wait(slot):
+        remote(x_ref, xb.at[slot], x_send.at[0], x_recv.at[slot], seq=inner).wait_recv()
+
+    row_at = lax.broadcasted_iota(jnp.int32, (tokens, tokens), 0)
+    col_at = lax.broadcasted_iota(jnp.int32, (tokens, tokens), 1)
+    earlier = (row_at < col_at).astype(F32).astype(BF16)
+    slots = lax.broadcasted_iota(jnp.int32, (capacity, tokens), 0).astype(F32)
+
+    def placing(block, expert):
+        info = block[tokens:tokens + 16, 0:tokens].astype(F32)
+        number = expert.astype(F32)
+        first = (info[0:1] == number).astype(F32)
+        second = (info[1:2] == number).astype(F32)
+        hit = first + second
+        gate = first * (info[2:3] + info[3:4] + info[4:5]) + second * (info[5:6] + info[6:7] + info[7:8])
+        hits = jnp.broadcast_to(hit, (16, tokens)).astype(BF16)
+        slot = jnp.dot(hits, earlier, preferred_element_type=F32)[0:1]
+        pick = jnp.where(slots == slot, 1.0, 0.0) * hit
+        return pick, jnp.sum(pick * gate, axis=1, keepdims=True)
+
+    def block_of(step):
+        return x_ref if step == 0 else xb.at[step]
+
+    def pick_rows(step):
+        block = block_of(step)
+        mine, _ = placing(block, s)
+        theirs, _ = placing(block, mate)
+        picked = jnp.dot(theirs.astype(BF16), block[0:tokens, :], preferred_element_type=F32)
+        rows_out[step] = picked.astype(BF16)
+        send(remote(rows_out.at[step], rows_in.at[step, 1], swap_send.at[step], swap_recv.at[step], seq=mate))
+        picked = jnp.dot(mine.astype(BF16), block[0:tokens, :], preferred_element_type=F32)
+        rows_in[step, 0] = picked.astype(BF16)
+
+    def gate_up(step):
+        remote(rows_out.at[step], rows_in.at[step, 1], swap_send.at[step], swap_recv.at[step], seq=mate).wait_recv()
+        rows = rows_in[step].reshape(2 * capacity, width)
+
+        @pl.loop(0, 4)
+        def _(q):
+            columns = pl.ds(pl.multiple_of(q * part, part), part)
+            gu[step, q, :, 0:part] = jnp.dot(rows, wg[:, columns], preferred_element_type=F32).astype(BF16)
+            gu[step, q, :, part:2 * part] = jnp.dot(rows, wu[:, columns], preferred_element_type=F32).astype(BF16)
+
+        for at, peer in enumerate(peers):
+            send(remote(gu.at[step, peer], gu_in.at[step, at], gu_send.at[step, at], gu_recv.at[step, at], head=peer))
+
+    def hidden(step):
+        total = gu[step, h].astype(F32)
+        for at, peer in enumerate(peers):
+            remote(gu.at[step, peer], gu_in.at[step, at], gu_send.at[step, at], gu_recv.at[step, at],
+                   head=peer).wait_recv()
+            total = total + gu_in[step, at].astype(F32)
+        gate = total[:, 0:part]
+        hid[step, h] = (gate / (1.0 + jnp.exp(-gate)) * total[:, part:2 * part]).astype(BF16)
+        for at, peer in enumerate(peers):
+            send(remote(hid.at[step, h], hid.at[step, h], hid_send.at[step, at], hid_recv.at[step, at], head=peer))
+
+    def down(step):
+        for at, peer in enumerate(peers):
+            remote(hid.at[step, peer], hid.at[step, peer], hid_send.at[step, at], hid_recv.at[step, at],
+                   head=peer).wait_recv()
+        total = jnp.dot(hid[step, 0], wd[0:part, :], preferred_element_type=F32)
+        for q in range(1, 4):
+            total = total + jnp.dot(hid[step, q], wd[q * part:(q + 1) * part, :], preferred_element_type=F32)
+        back_out[step] = total[capacity:].astype(BF16)
+        send(remote(back_out.at[step], back_in.at[step], back_send.at[step], back_recv.at[step], seq=mate))
+        near[step] = total[0:capacity].astype(BF16)
+
+    def combine(step):
+        block = block_of(step)
+        mine, mine_weight = placing(block, s)
+        theirs, theirs_weight = placing(block, mate)
+        first = (near[step].astype(F32) * mine_weight).astype(BF16)
+        value = jnp.dot(mine.T.astype(BF16), first, preferred_element_type=F32)
+        remote(back_out.at[step], back_in.at[step], back_send.at[step], back_recv.at[step], seq=mate).wait_recv()
+        second = (back_in[step].astype(F32) * theirs_weight).astype(BF16)
+        value = value + jnp.dot(theirs.T.astype(BF16), second, preferred_element_type=F32)
+        contrib[step] = value.astype(BF16)
+
+    pieces = CHAIN_PARTS
+    piece = width // pieces
+
+    def acc_copy(source, slot, at, to):
+        return remote(source, acc_in.at[slot, at], acc_send.at[slot, at], acc_recv.at[slot, at], seq=to)
+
+    def acc_wait(slot, at):
+        acc_copy(acc_out.at[0, at], slot, at, inner).wait_recv()
+
+    def cut(ref, at):
+        return ref[:, at * piece:(at + 1) * piece].astype(F32)
+
+    pick_rows(0)
+    for copy in loads[:2]:
+        copy.wait()
+    gate_up(0)
+    hidden(0)
+    loads[2].wait()
+    x_wait(1)
+    send_when(z == 1, remote(xb.at[1], xb.at[3], x_send.at[2], x_recv.at[3], seq=inner))
+    send_when(z == 2, remote(xb.at[1], xb.at[2], x_send.at[2], x_recv.at[2], seq=outer))
+    pl.when(middle)(lambda: x_wait(2))
+    send_when(z == 1, remote(xb.at[2], xb.at[2], x_send.at[3], x_recv.at[2], seq=outer))
+    send_when(z == 2, remote(xb.at[2], xb.at[3], x_send.at[3], x_recv.at[3], seq=inner))
+    pick_rows(1)
+    down(0)
+    gate_up(1)
+    combine(0)
+    hidden(1)
+    pl.when(edge)(lambda: x_wait(2))
+    pl.when(middle)(lambda: x_wait(3))
+    send_when(middle, remote(xb.at[3], xb.at[3], x_send.at[4], x_recv.at[3], seq=outer))
+    pick_rows(2)
+    down(1)
+    gate_up(2)
+    combine(1)
+
+    def put_pieces(slot, step):
+        for at in range(pieces):
+            acc_out[slot, at] = contrib[step, :, at * piece:(at + 1) * piece]
+
+    def from_edges(slot, step):
+        pl.when(edge)(lambda: put_pieces(slot, step))
+        for at in range(pieces):
+            send_when(edge, acc_copy(acc_out.at[slot, at], slot, at, inner))
+
+    from_edges(0, 1)
+    hidden(2)
+    pl.when(edge)(lambda: x_wait(3))
+    pick_rows(3)
+    down(2)
+    gate_up(3)
+    combine(2)
+    from_edges(1, 2)
+    hidden(3)
+
+    def add_second():
+        for at in range(pieces):
+            acc_wait(1, at)
+            here = jnp.where(z == 1, cut(contrib.at[2], at), cut(contrib.at[1], at))
+            acc_out[2, at] = (here + acc_in[1, at].astype(F32)).astype(BF16)
+
+    down(3)
+    combine(3)
+    from_edges(3, 3)
+    pl.when(middle)(add_second)
+    for at in range(pieces):
+        send_when(middle, acc_copy(acc_out.at[2, at], 2, at, inner))
+    for at in range(pieces):
+        def add_third(at=at):
+            acc_wait(3, at)
+            acc_out[4, at] = (cut(contrib.at[3], at) + acc_in[3, at].astype(F32)).astype(BF16)
+
+        pl.when(middle)(add_third)
+        send_when(middle, acc_copy(acc_out.at[4, at], 4, at, inner))
+    for at in range(pieces):
+        def add_last(at=at):
+            acc_wait(4, at)
+            here = jnp.where(z == 2, cut(contrib.at[2], at), cut(contrib.at[1], at))
+            acc_out[5, at] = (here + acc_in[4, at].astype(F32)).astype(BF16)
+
+        pl.when(middle)(add_last)
+        send_when(middle, acc_copy(acc_out.at[5, at], 5, at, outer))
+    for at in range(pieces):
+        span = slice(at * piece, (at + 1) * piece)
+
+        def finish_middle(at=at, span=span):
+            acc_wait(0, at)
+            acc_wait(2, at)
+            total = x_ref[0:tokens, span].astype(F32) + contrib[0, :, span].astype(F32)
+            total = total + acc_in[0, at].astype(F32) + acc_in[2, at].astype(F32)
+            out_ref[:, span] = total.astype(BF16)
+
+        pl.when(middle)(finish_middle)
+    for at in range(pieces):
+        span = slice(at * piece, (at + 1) * piece)
+
+        def finish_edge(at=at, span=span):
+            total = x_ref[0:tokens, span].astype(F32) + contrib[0, :, span].astype(F32)
+            acc_wait(5, at)
+            out_ref[:, span] = (total + acc_in[5, at].astype(F32)).astype(BF16)
+
+        pl.when(edge)(finish_edge)
+    for condition, copy in sent:
+        if condition is None:
+            copy.wait_send()
+        else:
+            pl.when(condition)(copy.wait_send)
+
+
+def experts_on_line(moe_in, expert_ids, gate_w, w_gate, w_up, w_down):
+    tokens, width = moe_in.shape
+    units = w_gate.shape[1]
+    capacity, part, pieces = tokens // 2, units // 4, CHAIN_PARTS
+    high = lax.reduce_precision(gate_w, 8, 7)
+    mid = lax.reduce_precision(gate_w - high, 8, 7)
+    low = gate_w - high - mid
+    info = jnp.stack(
+        [expert_ids[:, 0].astype(F32), expert_ids[:, 1].astype(F32)]
+        + [v[:, k] for k in (0, 1) for v in (high, mid, low)]
+    )
+    info = jnp.pad(info, ((0, 8), (0, width - tokens))).astype(BF16)
+    block = jnp.concatenate([moe_in, info], axis=0)
+    vmem, dma = pltpu.VMEM, pltpu.SemaphoreType.DMA
+    flops = 2 * 8 * capacity * width * units * 3
+    return pl.pallas_call(
+        functools.partial(experts_kernel, (tokens, width, capacity, part)),
+        out_shape=jax.ShapeDtypeStruct((tokens, width), BF16),
+        in_specs=[pl.BlockSpec(memory_space=pltpu.VMEM)] + [pl.BlockSpec(memory_space=pl.ANY)] * 3,
+        out_specs=pl.BlockSpec(memory_space=pltpu.VMEM),
+        scratch_shapes=[
+            vmem((width, units), BF16),
+            vmem((width, units), BF16),
+            vmem((units, width), BF16),
+            vmem((4, tokens + 16, width), BF16),
+            vmem((4, capacity, width), BF16),
+            vmem((4, 2, capacity, width), BF16),
+            vmem((4, 4, 2 * capacity, 2 * part), BF16),
+            vmem((4, 3, 2 * capacity, 2 * part), BF16),
+            vmem((4, 4, 2 * capacity, part), BF16),
+            vmem((4, capacity, width), BF16),
+            vmem((4, capacity, width), BF16),
+            vmem((4, capacity, width), BF16),
+            vmem((4, tokens, width), BF16),
+            vmem((6, pieces, tokens, width // pieces), BF16),
+            vmem((6, pieces, tokens, width // pieces), BF16),
+            dma((3,)),
+            dma((5,)),
+            dma((4,)),
+            dma((4,)),
+            dma((4,)),
+            dma((4, 3)),
+            dma((4, 3)),
+            dma((4, 3)),
+            dma((4, 3)),
+            dma((4,)),
+            dma((4,)),
+            dma((6, pieces)),
+            dma((6, pieces)),
+        ],
+        compiler_params=pltpu.CompilerParams(
+            collective_id=0, has_side_effects=True, vmem_limit_bytes=60 * 1024 * 1024
+        ),
+        cost_estimate=pl.CostEstimate(flops=flops, bytes_accessed=16 * 1024 * 1024, transcendentals=0),
+    )(block, w_gate, w_up, w_down)
+
+
 def on_device(
     q_nope,
     q_rope,
@@ -67,13 +380,22 @@
     tokens_here = moe_in.shape[0]
     feat_width = moe_in.shape[1]
     top_count = expert_ids.shape[1]
+    if (lax.axis_size("seq"), lax.axis_size("head"), top_count) == (8, 4, 2):
+        attn_out = attend_local(q_nope, q_rope, all_keys, key_ids, query_ids, w_uk, w_uv)
+        moe_out = experts_on_line(moe_in, expert_ids, gate_w, w_gate[0], w_up[0], w_down[0])
+        return (attn_out, moe_out)
     expert_count = lax.axis_size("seq")
     capacity = 2 * tokens_here * top_count // expert_count
     flat_ids = expert_ids.reshape(-1)
     onehot = (flat_ids[:, None] == jnp.arange(expert_count, dtype=jnp.int32)[None, :]).astype(
         jnp.int32
     )
-    before = jnp.cumsum(onehot, axis=0) - onehot
+    order = jnp.arange(flat_ids.shape[0], dtype=jnp.int32)
+    before = jnp.dot(
+        (order[None, :] < order[:, None]).astype(jnp.bfloat16),
+        onehot.astype(jnp.bfloat16),
+        preferred_element_type=jnp.float32,
+    ).astype(jnp.int32)
     slot_of = jnp.sum(before * onehot, axis=1)
     target = flat_ids * capacity + slot_of
     placing = (

time: 392 us -> 206 us (0.53)
  the two profiles are of different devices: /device:TPU:16 before, /device:TPU:0 now
where the time goes in v1:
time: 206 us; the launch traced here: 205 us
  Pallas kernels  164 us (80%)
  matrix products  23.8 us (12%)
  other arithmetic  8.39 us (4%)
  local copies, waits for them, and re-layouts  6.28 us (3%)
  starting transfers between devices  2.37 us (1%)
    pallas_call x1, Pallas kernels, experts_on_line(): pl.pallas_call(functools.partial(experts_kernel, (tokens, width, capacity...  164 us
    dot_general x1, matrix products, attend_local(): jnp.einsum('htl,hlv->thv', mixed_latent, w_uv, preferred_element_type=jnp...  13.3 us
    dot_general x1, matrix products, attend_local(): jnp.einsum('htl,kl->htk', q_latent, latent, preferred_element_type=jnp.fl...  7.79 us
    unnamed x8, local copies, waits for them, and re-layouts  4.71 us
    sub x1, other arithmetic, attend_local(): expo = jnp.exp(scores - highest)  4.64 us
  transfers between devices with their start and end apart: 1, of which 0 were waited for; matrix products, arithmetic and copies ran while one was open for 3% of the time, Pallas kernels for 80%

profile of v1, /device:TPU:0, one launch (start us, length us, event | category | flops | bytes accessed | tf_op | source)
XLA Modules:
  0.0 205.4 jit_solution(16812546209789446073)
XLA Ops:
  0.6 0.0 copy-start
  0.6 1.1 copy.21
  1.8 2.4 %collective-permute-start = (bf16[128,576]{1,0:T(8,128)(2,1)S(1)}, bf16[128,576]{1,0:T(8,128)(2,1)S(1)}, u32[]{:S(2)}, u32[]{:S(2)}) collective-permute-start(bf16[128,576]{1,0:T(8,128)(2,1)S(1)} %copy.21), channel_id=1, source_target_pairs={{0,1},{1,2},{2,3},{3,4},{4,5},{5,6},{6,7},{8,9},{9,10},{10,11},{11... | collective-permute-start | bytes 442376 | tf_op jit(solution)/shard_map/ppermute | solution.py:13
  4.2 0.8 pad_dynamic-slice_fusion
  5.0 0.8 dynamic_slice.7
  5.7 1.3 copy.23
  7.0 0.7 fusion.34
  7.7 0.8 convert_bitcast_fusion
  8.5 2.2 %fusion.23.x_ref = bf16[272,1792]{1,0:T(8,128)(2,1)} fusion(bf16[8,256]{1,0:T(8,128)(2,1)S(1)} %stack.6, bf16[256,1792]{1,0:T(8,128)(2,1)} %param.18), kind=kLoop, calls=%fused_computation.18 | loop fusion | flops 2924544 | bytes 1896448 | tf_op jit(solution)/shard_map/concatenate | solution.py:314
  10.7 163.9 %shard_map.131 = bf16[256,1792]{1,0:T(8,128)(2,1)} custom-call(bf16[272,1792]{1,0:T(8,128)(2,1)} %fusion.23.x_ref, bf16[1792,1024]{1,0:T(8,128)(2,1)} %bitcast.53, bf16[1792,1024]{1,0:T(8,128)(2,1)} %bitcast.54, bf16[1024,1792]{1,0:T(8,128)(2,1)} %bitcast.55), custom_call_target="tpu_custom_call" | custom-call | flops 11274289152 | bytes 16777216 | tf_op jit(solution)/shard_map/pallas_call | solution.py:317
  174.6 0.1 fusion.26
  174.8 0.0 collective-permute-done
  174.8 2.7 %fusion.28 = f32[256,128,32]{0,1,2:T(8,128)} fusion(bf16[128,32,64]{0,2,1:T(8,128)(2,1)S(1)} %bitcast.51, bf16[128,576]{1,0:T(8,128)(2,1)S(1)} %copy.21, bf16[128,576]{1,0:T(8,128)(2,1)S(1)} %collective-permute-done), kind=kOutput, calls=%fused_computation.27 | convolution fusion | flops 134283264 | bytes 5013504 | tf_op jit(solution)/shard_map/thr,kr->htk/dot_general | solution.py:32
  177.4 0.0 copy-done
  177.4 7.8 %fusion.2 = f32[32,128,256]{2,1,0:T(8,128)} fusion(f32[256,128,32]{0,1,2:T(8,128)} %fusion.28, bf16[32,128,512]{2,1,0:T(8,128)(2,1)} %param.16, pred[128,256]{1,0:T(8,128)(4,1)S(1)} %fusion.26, bf16[128,576]{1,0:T(8,128)(2,1)S(1)} %collective-permute-done, bf16[128,576]{1,0:T(8,128)(2,1)S(1)} %copy.21, bf16[128,4096]{1,0:T(8,128)(2,1)S(1)} %copy-done), kind=kOutput, calls=%fused_computation.3 | convolution fusion | flops 1616379904 | bytes 13959168 | tf_op jit(solution)/shard_map/htl,kl->htk/dot_general | solution.py:30
  185.2 4.6 %fusion.41 = f32[32,128]{1,0:T(8,128)S(1)} fusion(f32[32,128,256]{2,1,0:T(8,128)} %fusion.2), kind=kOutput, calls=%fused_computation.48 | output fusion | flops 2097407 | bytes 4210688 | tf_op jit(solution)/shard_map/sub | solution.py:40
  189.9 0.0 copy-start.1
  189.9 13.3 %fusion.16 = bf16[32,128,128]{1,2,0:T(8,128)(2,1)S(1)} fusion(bf16[32,512,128]{2,1,0:T(8,128)(2,1)} %param.17, f32[32,128]{1,0:T(8,128)S(1)} %fusion.41, f32[32,128,256]{2,1,0:T(8,128)} %fusion.2, bf16[128,576]{1,0:T(8,128)(2,1)S(1)} %collective-permute-done, bf16[128,576]{1,0:T(8,128)(2,1)S(1)} %copy.21), kind=kOutput, calls=%fused_computation.15 | convolution fusion | flops 1616908544 | bytes 13942784 | tf_op jit(solution)/shard_map/htl,hlv->thv/dot_general | solution.py:45
  203.2 1.3 copy.27
  204.5 0.0 copy-done.1
  204.5 0.9 copy.40
  (4 shorter events, 0.0 us)
Async XLA Ops:
  0.6 176.8 %copy-start = (bf16[128,4096]{1,0:T(8,128)(2,1)S(1)}, bf16[128,4096]{1,0:T(8,128)(2,1)}, u32[]{:S(2)}) copy-start(bf16[128,4096]{1,0:T(8,128)(2,1)} %param.12) | copy-start | bytes 3145732
  1.8 173.0 %collective-permute-start = (bf16[128,576]{1,0:T(8,128)(2,1)S(1)}, bf16[128,576]{1,0:T(8,128)(2,1)S(1)}, u32[]{:S(2)}, u32[]{:S(2)}) collective-permute-start(bf16[128,576]{1,0:T(8,128)(2,1)S(1)} %copy.21), channel_id=1, source_target_pairs={{0,1},{1,2},{2,3},{3,4},{4,5},{5,6},{6,7},{8,9},{9,10},{10,11},{11... | collective-permute-start | bytes 442376 | tf_op jit(solution)/shard_map/ppermute | solution.py:13
  189.9 14.6 %copy-start.1 = (bf16[256,1792]{1,0:T(8,128)(2,1)S(1)}, bf16[256,1792]{1,0:T(8,128)(2,1)}, u32[]{:S(2)}) copy-start(bf16[256,1792]{1,0:T(8,128)(2,1)} %shard_map.131) | copy-start | bytes 2752516
